TPU v7x, 32 devices: a whole 2x2x4 slice. The times are simulated.
32 devices in a mesh: replica: 16 (over z, y, core), tensor: 2 (over x).
Axes of the slice: x: 2, y: 2, z: 4, core: 2. Of those that a mesh axis runs over, the one named last changes fastest.
Arguments:
- prefill_q: bfloat16 [6144, 8192], P('replica', 'tensor'), may hold values from -16 to 16
- decode_q: bfloat16 [32, 8192], P('replica', 'tensor'), may hold values from -16 to 16
- overflow_q: bfloat16 [96, 8192], P('replica', 'tensor'), may hold values from -16 to 16
- key_pool: bfloat16 [67584, 1024], P('replica', 'tensor'), may hold values from -10 to 10
- value_pool: bfloat16 [67584, 1024], P('replica', 'tensor'), may hold values from -6 to 6
- prefill_pages: int32 [16, 19], P('replica'), may hold values from 0 to 32, as said below
- decode_pages: int32 [32, 4], P('replica'), may hold values from 0 to 32, as said below
- decode_len: int32 [32], P('replica'), may hold values from 1 to 512, as said below
- overflow_pages: int32 [96], P('replica'), may hold values from 0 to 32, as said below
- overflow_len: int32 [96], P('replica'), may hold values from 1 to 128, as said below
- overflow_dest: int32 [96], P('replica'), may hold values from 0 to 15, as said below
Outputs:
- prefill_out: bfloat16 [6144, 8192], P(('replica', 'tensor'))
- decode_out: bfloat16 [32, 8192], P('replica', 'tensor')
- moved_out: bfloat16 [256, 8192], P('replica', 'tensor')
Inputs may be any that keep to these rules, and one draw needn't show every extreme that they name: The page lists of one replica (prefill_pages, decode_pages and overflow_pages together) name distinct pages of that replica's pool. `decode_pages`: distinct pages of the own pool, as for prefill_pages. `overflow_pages`: distinct pages of the own pool, as for prefill_pages. `decode_len`: every replica has a decoding request of exactly 512 positions. `overflow_len`: every replica has an overflow request of exactly 128 positions. `overflow_dest`: the requests of one replica go to distinct replicas other than itself; one replica receives a request from every other replica.
All inputs are finite; a program needn't handle non-finite values.
Results may differ from a plain program's by a relative error of at most 0.0049.
Values may be sent and summed in bfloat16 or wider, within the bound.
No kernel may reach another device: no remote copies, remote signals or barrier semaphores. Data moves between devices by JAX's collectives and lax.ppermute only.
A program may use at most 128 MiB of HBM per device.

v0:
```python
import functools
import math

import jax
import jax.numpy as jnp
from jax import lax
from jax.experimental import pallas as pl
from jax.experimental.pallas import tpu as pltpu
from jax.sharding import PartitionSpec as P

Q_HEADS = 64
KV_HEADS = 8
D_HEAD = 128
PAGE = 128
GROUP = Q_HEADS // KV_HEADS
SCALE = math.log2(math.e) / math.sqrt(D_HEAD)
LOW = -1e30
CHUNK = 512
PACK = 2
VMEM_LIMIT = 60 * 2**20

NT = (((1,), (1,)), ((), ()))


def chunks_of(earlier, tail):
    starts = list(range(0, earlier, CHUNK)) + [earlier]
    return [(a, b - a) for a, b in zip(starts, starts[1:] + [earlier + tail])]


def prefill_kernel(
    tail, blk_ref, pages_ref, q_ref, k_hbm, v_hbm, o_ref,
    kbuf, vbuf, score_a, score_b, top_a, top_b, sem, *, first
):
    heads = kbuf.shape[0]
    count = pages_ref.shape[0]
    span = count * PAGE
    rows = q_ref.shape[0]
    units = GROUP // PACK
    pieces = chunks_of(span - tail, tail)

    def fetch(head):
        cols = pl.ds(pl.multiple_of((first + head) * D_HEAD, D_HEAD), D_HEAD)

        def one(j, _):
            src = pl.ds(pl.multiple_of(pages_ref[j] * PAGE, PAGE), PAGE)
            dst = pl.ds(pl.multiple_of(j * PAGE, PAGE), PAGE)
            pltpu.make_async_copy(k_hbm.at[src, cols], kbuf.at[head, dst], sem.at[head, 0]).start()
            pltpu.make_async_copy(v_hbm.at[src, cols], vbuf.at[head, dst], sem.at[head, 1]).start()
            return 0

        lax.fori_loop(0, count, one, 0)

    def ready(head):
        pltpu.make_async_copy(kbuf.at[head], kbuf.at[head], sem.at[head, 0]).wait()
        pltpu.make_async_copy(vbuf.at[head], vbuf.at[head], sem.at[head, 1]).wait()

    def columns(unit, h):
        return pl.ds(pl.multiple_of((unit * PACK + h) * D_HEAD, D_HEAD), D_HEAD)

    def across(x, size):
        return jnp.concatenate([x] * (size // D_HEAD), axis=1)

    def run(now, later):
        if later is not None:
            unit, score, top = later
            head = unit // units
            q = jnp.concatenate([q_ref[:, columns(unit, h)] for h in range(PACK)], axis=0)
            best = None
        if now is not None:
            unit_now, score_now, top_now = now
            head_now = unit_now // units
            shift = top_now[...]
            acc = None
        for start, size in pieces:
            if later is not None:
                keys = kbuf[head, start:start + size, :]
                s = lax.dot_general(q, keys, NT, preferred_element_type=jnp.float32)
                if start >= span - tail:
                    usable = lax.broadcasted_iota(jnp.int32, (rows, size), 1) <= (
                        lax.broadcasted_iota(jnp.int32, (rows, size), 0) + blk_ref[0] * rows
                    )
                    s = jnp.where(usable[None], s.reshape(PACK, rows, size), LOW).reshape(s.shape)
                score[:, start:start + size] = s
                for at in range(0, size, D_HEAD):
                    piece = s[:, at:at + D_HEAD]
                    best = piece if best is None else jnp.maximum(best, piece)
            if now is not None:
                p = jnp.exp2(score_now[:, start:start + size] * SCALE - across(shift, size))
                values = vbuf[head_now, start:start + size, :]
                wide = jnp.concatenate([values, jnp.ones_like(values)], axis=1)
                o = jnp.dot(p.astype(jnp.bfloat16), wide, preferred_element_type=jnp.float32)
                acc = o if acc is None else acc + o
        if later is not None:
            top[...] = jnp.broadcast_to(jnp.max(best, axis=1, keepdims=True) * SCALE, top.shape)
        if now is not None:
            o = (acc[:, :D_HEAD] / acc[:, D_HEAD:]).astype(o_ref.dtype)
            for h in range(PACK):
                o_ref[:, columns(unit_now, h)] = o[h * rows:(h + 1) * rows]

    fetch(0)
    if heads > 1:
        fetch(1)
    ready(0)
    a, b = (score_a, top_a), (score_b, top_b)
    run(None, (0, *a))

    def body(i, _):
        u = 2 * i
        run((u, *a), (u + 1, *b))
        if heads > 1:
            head = (u + 2) // units

            @pl.when(((u + 2) % units == 0) & (head < heads))
            def _():
                @pl.when(head + 1 < heads)
                def _():
                    fetch(head + 1)

                ready(head)

        run((u + 1, *b), (jnp.minimum(u + 2, heads * units - 1), *a))
        return 0

    lax.fori_loop(0, heads * units // 2, body, 0)


def prefill_part(q, keys, values, pages, blk, ranks, first, heads, wide=False):
    tokens = q.shape[0]
    rows = tokens // ranks
    span = pages.shape[0] * PAGE
    width = heads * GROUP * D_HEAD
    total = ranks * keys.shape[1] // D_HEAD // heads if wide else 1
    work = heads * GROUP * rows * span

    return pl.pallas_call(
        functools.partial(prefill_kernel, tokens, first=first),
        grid_spec=pltpu.PrefetchScalarGridSpec(
            num_scalar_prefetch=2,
            grid=(1,),
            in_specs=[
                pl.BlockSpec((rows, width), lambda i, blk, pages: (blk[0], first // heads)),
                pl.BlockSpec(memory_space=pl.ANY),
                pl.BlockSpec(memory_space=pl.ANY),
            ],
            out_specs=pl.BlockSpec((rows, width), lambda i, blk, pages: (0, blk[0] if wide else 0)),
            scratch_shapes=[
                pltpu.VMEM((heads, span, D_HEAD), jnp.bfloat16),
                pltpu.VMEM((heads, span, D_HEAD), jnp.bfloat16),
                pltpu.VMEM((PACK * rows, span), jnp.float32),
                pltpu.VMEM((PACK * rows, span), jnp.float32),
                pltpu.VMEM((PACK * rows, D_HEAD), jnp.float32),
                pltpu.VMEM((PACK * rows, D_HEAD), jnp.float32),
                pltpu.SemaphoreType.DMA((heads, 2)),
            ],
        ),
        out_shape=jax.ShapeDtypeStruct((rows, total * width), q.dtype),
        compiler_params=pltpu.CompilerParams(vmem_limit_bytes=VMEM_LIMIT),
        cost_estimate=pl.CostEstimate(
            flops=4 * work * D_HEAD,
            bytes_accessed=4 * (heads * span * D_HEAD + rows * width),
            transcendentals=work,
        ),
        name="prefill",
    )(blk, pages, q, keys, values)


def small_kernel(
    dec, over, pages_ref, len_ref, dest_ref, q_ref, k_hbm, v_hbm, dec_ref, out_ref,
    kbuf, vbuf, res, sem
):
    count = pages_ref.shape[0]
    batch = q_ref.shape[0]
    per = (count - over) // dec
    keys = count * PAGE

    def one(j, _):
        src = pl.ds(pl.multiple_of(pages_ref[j] * PAGE, PAGE), PAGE)
        dst = pl.ds(pl.multiple_of(j * PAGE, PAGE), PAGE)
        pltpu.make_async_copy(k_hbm.at[src], kbuf.at[dst], sem.at[0]).start()
        pltpu.make_async_copy(v_hbm.at[src], vbuf.at[dst], sem.at[1]).start()
        return 0

    lax.fori_loop(0, count, one, 0)
    row = lax.broadcasted_iota(jnp.int32, (batch, PAGE), 0)
    lane = lax.broadcasted_iota(jnp.int32, (batch, PAGE), 1)
    masks = []
    for j in range(count):
        owner, base = (j, 0) if j < over else (over + (j - over) // per, (j - over) % per * PAGE)
        masks.append((row == owner) & (lane + base < len_ref[owner]))
    pltpu.make_async_copy(kbuf, kbuf, sem.at[0]).wait()
    pltpu.make_async_copy(vbuf, vbuf, sem.at[1]).wait()
    for g in range(k_hbm.shape[1] // D_HEAD):
        cols = slice(g * D_HEAD, (g + 1) * D_HEAD)
        q = jnp.concatenate(
            [q_ref[:, (g * GROUP + h) * D_HEAD:(g * GROUP + h + 1) * D_HEAD] for h in range(GROUP)],
            axis=0,
        ).astype(jnp.bfloat16)
        s = lax.dot_general(q, kbuf[:, cols], NT, preferred_element_type=jnp.float32)
        s = s.reshape(GROUP, batch, keys)
        s = jnp.concatenate(
            [
                jnp.where(masks[j][None], s[:, :, j * PAGE:(j + 1) * PAGE], LOW)
                for j in range(count)
            ],
            axis=2,
        ).reshape(GROUP * batch, keys)
        p = jnp.exp2((s - jnp.max(s, axis=1, keepdims=True)) * SCALE)
        total = jnp.sum(p, axis=1, keepdims=True)
        w = (p / total).astype(jnp.bfloat16)
        o = jnp.dot(w, vbuf[:, cols], preferred_element_type=jnp.float32)
        for h in range(GROUP):
            at = (g * GROUP + h) * D_HEAD
            res[:, at:at + D_HEAD] = o[h * batch:(h + 1) * batch]
    width = q_ref.shape[1]
    dec_ref[...] = res[over:over + dec, :].astype(dec_ref.dtype)
    lines = out_ref.shape[0]
    line = lax.broadcasted_iota(jnp.int32, (lines, D_HEAD), 0)
    where_to = jnp.full((lines, D_HEAD), -1, jnp.int32)
    for m in range(over):
        where_to = jnp.where(line == m, dest_ref[m], where_to)
    out_ref[:, width:] = where_to.astype(jnp.float32).astype(out_ref.dtype)
    real = lax.broadcasted_iota(jnp.int32, (lines, width), 0) < over
    out_ref[:, :width] = jnp.where(real, res[0:lines, :], 0.0).astype(out_ref.dtype)


def small_part(decode_q, overflow_q, keys, values, pages, lens, dest):
    dec, over = decode_q.shape[0], overflow_q.shape[0]
    lines = -(-over // 8) * 8
    batch = -(-(dec + over) // 8) * 8
    width = decode_q.shape[1]
    q = jnp.concatenate([overflow_q, decode_q], axis=0).astype(jnp.float32)
    q = jnp.pad(q, ((0, batch - dec - over), (0, 0)))
    span = pages.shape[0] * PAGE
    work = batch * width * span
    return pl.pallas_call(
        functools.partial(small_kernel, dec, over),
        grid_spec=pltpu.PrefetchScalarGridSpec(
            num_scalar_prefetch=3,
            grid=(1,),
            in_specs=[
                pl.BlockSpec((batch, width), lambda i, *_: (0, 0)),
                pl.BlockSpec(memory_space=pl.ANY),
                pl.BlockSpec(memory_space=pl.ANY),
            ],
            out_specs=[
                pl.BlockSpec((dec, width), lambda i, *_: (0, 0)),
                pl.BlockSpec((lines, width + D_HEAD), lambda i, *_: (0, 0)),
            ],
            scratch_shapes=[
                pltpu.VMEM((span, keys.shape[1]), jnp.bfloat16),
                pltpu.VMEM((span, keys.shape[1]), jnp.bfloat16),
                pltpu.VMEM((batch, width), jnp.float32),
                pltpu.SemaphoreType.DMA((2,)),
            ],
        ),
        out_shape=[
            jax.ShapeDtypeStruct((dec, width), decode_q.dtype),
            jax.ShapeDtypeStruct((lines, width + D_HEAD), decode_q.dtype),
        ],
        compiler_params=pltpu.CompilerParams(vmem_limit_bytes=VMEM_LIMIT),
        cost_estimate=pl.CostEstimate(
            flops=4 * work, bytes_accessed=4 * span * keys.shape[1], transcendentals=work // D_HEAD
        ),
        name="small",
    )(pages, lens, dest, q, keys, values)


def finish_kernel(me_ref, at_ref, all_ref, big_ref, *refs):
    got, (out_ref, mov_ref, sem) = refs[:-3], refs[-3:]
    del big_ref
    cols = GROUP * D_HEAD
    copies = []
    for i, part in enumerate(got):
        to = pl.ds(pl.multiple_of(at_ref[i] * cols, cols), cols)
        copies.append(pltpu.make_async_copy(part, out_ref.at[:, to], sem.at[i]))
        copies[-1].start()
    replicas, width = mov_ref.shape
    lines = all_ref.shape[1]
    table = all_ref[...].astype(jnp.float32).reshape(replicas * lines, width + D_HEAD)
    mine = table[:, width:width + 1] == me_ref[0].astype(jnp.float32)
    row = lax.broadcasted_iota(jnp.int32, (replicas * lines, replicas), 0)
    col = lax.broadcasted_iota(jnp.int32, (replicas * lines, replicas), 1)
    ours = mine & (row >= col * lines) & (row < (col + 1) * lines)
    pick = jnp.where(ours, 1.0, 0.0).astype(jnp.bfloat16)
    mov_ref[...] = lax.dot_general(
        pick,
        table[:, :width].astype(jnp.bfloat16),
        (((0,), (0,)), ((), ())),
        preferred_element_type=jnp.float32,
    ).astype(mov_ref.dtype)
    for copy in copies:
        copy.wait()


def finish_part(me, at, everyone, big, got):
    replicas, lines, width = everyone.shape
    width -= D_HEAD
    anywhere = pl.BlockSpec(memory_space=pl.ANY)
    return pl.pallas_call(
        finish_kernel,
        grid_spec=pltpu.PrefetchScalarGridSpec(
            num_scalar_prefetch=2,
            grid=(1,),
            in_specs=[pl.BlockSpec(everyone.shape, lambda i, *_: (0, 0, 0)), anywhere]
            + [pl.BlockSpec(memory_space=pltpu.VMEM)] * len(got),
            out_specs=[anywhere, pl.BlockSpec((replicas, width), lambda i, *_: (0, 0))],
            scratch_shapes=[pltpu.SemaphoreType.DMA((len(got),))],
        ),
        out_shape=[
            jax.ShapeDtypeStruct(big.shape, big.dtype),
            jax.ShapeDtypeStruct((replicas, width), big.dtype),
        ],
        input_output_aliases={3: 0},
        compiler_params=pltpu.CompilerParams(vmem_limit_bytes=VMEM_LIMIT),
        cost_estimate=pl.CostEstimate(
            flops=0, bytes_accessed=2 * big.size + 2 * everyone.size, transcendentals=0
        ),
        name="finish",
    )(me, at, everyone, big, *got)


def per_device(
    prefill_q,
    decode_q,
    overflow_q,
    key_pool,
    value_pool,
    prefill_pages,
    decode_pages,
    decode_len,
    overflow_pages,
    overflow_len,
    overflow_dest,
):
    ranks = lax.axis_size("tensor")
    rank = lax.axis_index("tensor")
    heads = key_pool.shape[1] // D_HEAD
    pages = prefill_pages[0]

    decode_out, sent = small_part(
        decode_q,
        overflow_q,
        key_pool,
        value_pool,
        jnp.concatenate([overflow_pages, decode_pages.reshape(-1)]),
        jnp.concatenate([overflow_len, decode_len]),
        overflow_dest,
    )
    everyone = lax.all_gather(sent, "replica", axis=0, tiled=False)

    got, at = [], []
    for shift in range(1, ranks):
        blk = lax.rem(rank + shift, ranks)[None].astype(jnp.int32)
        source = lax.rem(rank + ranks - shift, ranks)
        for g in range(heads):
            part = prefill_part(prefill_q, key_pool, value_pool, pages, blk, ranks, g, 1)
            got.append(lax.ppermute(part, "tensor", [(i, (i + shift) % ranks) for i in range(ranks)]))
            at.append(source * heads + g)
    prefill_out = prefill_part(
        prefill_q, key_pool, value_pool, pages, rank[None].astype(jnp.int32), ranks, 0, heads, wide=True
    )
    me = lax.axis_index("replica")[None].astype(jnp.int32)
    prefill_out, moved_out = finish_part(
        me, jnp.stack(at).astype(jnp.int32), everyone, prefill_out, got
    )
    return (prefill_out, decode_out, moved_out)


def solution(mesh):
    in_specs = (
        P("replica", "tensor"),
        P("replica", "tensor"),
        P("replica", "tensor"),
        P("replica", "tensor"),
        P("replica", "tensor"),
        P("replica", None),
        P("replica", None),
        P("replica"),
        P("replica"),
        P("replica"),
        P("replica"),
    )
    out_specs = (P(("replica", "tensor"), None), P("replica", "tensor"), P("replica", "tensor"))
    return jax.shard_map(
        per_device, mesh=mesh, in_specs=in_specs, out_specs=out_specs, check_vma=False
    )
```

profile of v0, /device:TPU:0, one launch (start us, length us, event | category | flops | bytes accessed | tf_op | source)
XLA Modules:
  0.0 105.1 jit_solution(9717115592853995237)
XLA Ops:
  7.2 0.0 all-gather.3.cloned.1.call-start
  7.2 0.8 reshape.9
  8.0 1.2 %pad_add_fusion.1.pages_ref = s32[14]{0:T(128)} fusion(s32[8]{0:T(128)S(1)} %reshape.9, s32[6]{0:T(128)} %param.19), kind=kLoop, calls=%fused_computation.2 | loop fusion | flops 14 | bytes 112 | tf_op jit(solution)/shard_map/concatenate | solution.py:345
  9.2 1.3 %pad_add_fusion.2.len_ref = s32[8]{0:T(128)} fusion(s32[2]{0:T(128)} %param.18, s32[6]{0:T(128)} %param.20), kind=kLoop, calls=%fused_computation.3 | loop fusion | flops 8 | bytes 64 | tf_op jit(solution)/shard_map/concatenate | solution.py:346
  10.5 1.5 %maximum_convert_fusion.q_ref = f32[8,4096]{1,0:T(8,128)} fusion(bf16[2,4096]{1,0:T(2,128)(2,1)} %param.12, bf16[6,4096]{1,0:T(8,128)(2,1)} %param.13), kind=kLoop, calls=%fused_computation | loop fusion | flops 131072 | bytes 196608 | tf_op jit(solution)/shard_map/convert_element_type | solution.py:231
  12.0 6.6 %small.1 = (bf16[2,4096]{1,0:T(2,128)(2,1)}, bf16[8,4224]{1,0:T(8,128)(2,1)}) custom-call(s32[14]{0:T(128)} %pad_add_fusion.1.pages_ref, s32[8]{0:T(128)} %pad_add_fusion.2.len_ref, s32[6]{0:T(128)} %dest_ref.1, f32[8,4096]{1,0:T(8,128)} %maximum_convert_fusion.q_ref, bf16[4224,512]{1,0:T(8,128)(2,1)} %k_hbm.11, bf16[4224,512]{1,0:T(8,128)(2,1)} %v_hbm.11), custom_call_target="tpu_custom_call" | custom-call | flops 234881024 | bytes 3670016 | tf_op jit(solution)/shard_map/small/pallas_call | solution.py:235
  18.7 0.0 all-gather.3.cloned.1.call-update
  18.7 9.1 %prefill.6 = bf16[192,1024]{1,0:T(8,128)(2,1)} custom-call(s32[1]{0:T(128)} %bitcast.8.blk_ref, s32[19]{0:T(128)} %bitcast.10, bf16[384,4096]{1,0:T(8,128)(2,1)} %q_ref.9, bf16[4224,512]{1,0:T(8,128)(2,1)} %k_hbm.11, bf16[4224,512]{1,0:T(8,128)(2,1)} %v_hbm.11), custom_call_target="tpu_custom_call" | custom-call | flops 1912602624 | bytes 2031616 | tf_op jit(solution)/shard_map/prefill/pallas_call | solution.py:135
  27.8 3.0 %collective-permute-start = (bf16[192,1024]{1,0:T(8,128)(2,1)}, bf16[192,1024]{1,0:T(8,128)(2,1)S(1)}, u32[]{:S(2)}, u32[]{:S(2)}) collective-permute-start(bf16[192,1024]{1,0:T(8,128)(2,1)} %prefill.6), channel_id=1, source_target_pairs={{0,1},{1,0},{2,3},{3,2},{4,5},{5,4},{6,7},{7,6},{8,9},{9,8},{10,11... | collective-permute-start | bytes 1179656 | tf_op jit(solution)/shard_map/ppermute | solution.py:357
  30.8 9.2 %prefill.7 = bf16[192,1024]{1,0:T(8,128)(2,1)} custom-call(s32[1]{0:T(128)} %bitcast.8.blk_ref, s32[19]{0:T(128)} %bitcast.11, bf16[384,4096]{1,0:T(8,128)(2,1)} %q_ref.9, bf16[4224,512]{1,0:T(8,128)(2,1)} %k_hbm.11, bf16[4224,512]{1,0:T(8,128)(2,1)} %v_hbm.11), custom_call_target="tpu_custom_call" | custom-call | flops 1912602624 | bytes 2031616 | tf_op jit(solution)/shard_map/prefill/pallas_call | solution.py:135
  40.0 0.1 collective-permute-start.1
  40.1 9.1 %prefill.8 = bf16[192,1024]{1,0:T(8,128)(2,1)} custom-call(s32[1]{0:T(128)} %bitcast.8.blk_ref, s32[19]{0:T(128)} %bitcast.12, bf16[384,4096]{1,0:T(8,128)(2,1)} %q_ref.9, bf16[4224,512]{1,0:T(8,128)(2,1)} %k_hbm.11, bf16[4224,512]{1,0:T(8,128)(2,1)} %v_hbm.11), custom_call_target="tpu_custom_call" | custom-call | flops 1912602624 | bytes 2031616 | tf_op jit(solution)/shard_map/prefill/pallas_call | solution.py:135
  49.2 2.1 %collective-permute-start.2 = (bf16[192,1024]{1,0:T(8,128)(2,1)}, bf16[192,1024]{1,0:T(8,128)(2,1)S(1)}, u32[]{:S(2)}, u32[]{:S(2)}) collective-permute-start(bf16[192,1024]{1,0:T(8,128)(2,1)} %prefill.8), channel_id=1, source_target_pairs={{0,1},{1,0},{2,3},{3,2},{4,5},{5,4},{6,7},{7,6},{8,9},{9,8},{10,11... | collective-permute-start | bytes 1179656 | tf_op jit(solution)/shard_map/ppermute | solution.py:357
  51.3 9.3 %prefill.9 = bf16[192,1024]{1,0:T(8,128)(2,1)} custom-call(s32[1]{0:T(128)} %bitcast.8.blk_ref, s32[19]{0:T(128)} %bitcast.13, bf16[384,4096]{1,0:T(8,128)(2,1)} %q_ref.9, bf16[4224,512]{1,0:T(8,128)(2,1)} %k_hbm.11, bf16[4224,512]{1,0:T(8,128)(2,1)} %v_hbm.11), custom_call_target="tpu_custom_call" | custom-call | flops 1912602624 | bytes 2031616 | tf_op jit(solution)/shard_map/prefill/pallas_call | solution.py:135
  60.6 0.1 collective-permute-start.3
  60.7 31.5 %prefill.5.big_ref = bf16[192,8192]{1,0:T(8,128)(2,1)} custom-call(s32[1]{0:T(128)} %bitcast.6.blk_ref, s32[19]{0:T(128)} %bitcast.14, bf16[384,4096]{1,0:T(8,128)(2,1)} %q_ref.9, bf16[4224,512]{1,0:T(8,128)(2,1)} %k_hbm.11, bf16[4224,512]{1,0:T(8,128)(2,1)} %v_hbm.11), custom_call_target="tpu_custom_call" | custom-call | flops 7650410496 | bytes 8126464 | tf_op jit(solution)/shard_map/prefill/pallas_call | solution.py:135
  92.2 0.6 pad_add_fusion.at_ref
  92.8 0.0 collective-permute-done.refs_0_
  92.8 0.0 copy-start
  92.8 0.0 collective-permute-done.1.refs_1_
  92.8 0.0 copy-start.1
  92.9 0.0 collective-permute-done.2.refs_2_
  92.9 0.0 copy-start.2
  92.9 0.0 collective-permute-done.3.refs_3_
  92.9 0.0 copy-start.3
  92.9 0.0 all-gather.3.cloned.1.call-done
  92.9 0.7 copy-done
  93.6 0.2 copy-done.1
  93.7 0.1 copy-done.2
  93.9 0.2 copy-done.3
  94.0 4.2 %finish.1 = (bf16[192,8192]{1,0:T(8,128)(2,1)}, bf16[16,4096]{1,0:T(8,128)(2,1)}) custom-call(s32[1]{0:T(128)} %bitcast.me_ref, s32[4]{0:T(128)} %pad_add_fusion.at_ref, bf16[16,8,4224]{2,1,0:T(8,128)(2,1)} %bitcast.9, bf16[192,8192]{1,0:T(8,128)(2,1)} %prefill.5.big_ref, bf16[192,1024]{1,0:T(8,128)(2,1)} %copy-done, ...), custom_call_target="tpu_custom_call", output_to_operand_aliasing={{0}: (3, {})} | custom-call | bytes 4227072 | tf_op jit(solution)/shard_map/finish/pallas_call | solution.py:299
Async XLA Ops:
  7.2 85.8 %all-gather.3.cloned.1.call-start = ((), (), s32[]{:S(2)}) async-start(), calls=%async_computation | async-start | bytes 1148928 | tf_op jit(solution)/shard_map/all_gather | solution.py:349
  27.8 65.0 %collective-permute-start = (bf16[192,1024]{1,0:T(8,128)(2,1)}, bf16[192,1024]{1,0:T(8,128)(2,1)S(1)}, u32[]{:S(2)}, u32[]{:S(2)}) collective-permute-start(bf16[192,1024]{1,0:T(8,128)(2,1)} %prefill.6), channel_id=1, source_target_pairs={{0,1},{1,0},{2,3},{3,2},{4,5},{5,4},{6,7},{7,6},{8,9},{9,8},{10,11... | collective-permute-start | bytes 1179656 | tf_op jit(solution)/shard_map/ppermute | solution.py:357
  40.0 52.8 %collective-permute-start.1 = (bf16[192,1024]{1,0:T(8,128)(2,1)}, bf16[192,1024]{1,0:T(8,128)(2,1)S(1)}, u32[]{:S(2)}, u32[]{:S(2)}) collective-permute-start(bf16[192,1024]{1,0:T(8,128)(2,1)} %prefill.7), channel_id=1, source_target_pairs={{0,1},{1,0},{2,3},{3,2},{4,5},{5,4},{6,7},{7,6},{8,9},{9,8},{10,11... | collective-permute-start | bytes 1179656 | tf_op jit(solution)/shard_map/ppermute | solution.py:357
  49.2 43.6 %collective-permute-start.2 = (bf16[192,1024]{1,0:T(8,128)(2,1)}, bf16[192,1024]{1,0:T(8,128)(2,1)S(1)}, u32[]{:S(2)}, u32[]{:S(2)}) collective-permute-start(bf16[192,1024]{1,0:T(8,128)(2,1)} %prefill.8), channel_id=1, source_target_pairs={{0,1},{1,0},{2,3},{3,2},{4,5},{5,4},{6,7},{7,6},{8,9},{9,8},{10,11... | collective-permute-start | bytes 1179656 | tf_op jit(solution)/shard_map/ppermute | solution.py:357
  60.6 32.2 %collective-permute-start.3 = (bf16[192,1024]{1,0:T(8,128)(2,1)}, bf16[192,1024]{1,0:T(8,128)(2,1)S(1)}, u32[]{:S(2)}, u32[]{:S(2)}) collective-permute-start(bf16[192,1024]{1,0:T(8,128)(2,1)} %prefill.9), channel_id=1, source_target_pairs={{0,1},{1,0},{2,3},{3,2},{4,5},{5,4},{6,7},{7,6},{8,9},{9,8},{10,11... | collective-permute-start | bytes 1179656 | tf_op jit(solution)/shard_map/ppermute | solution.py:357
  92.8 0.7 copy-start
  92.8 0.9 copy-start.1
  92.9 1.0 copy-start.2
  92.9 1.1 %copy-start.3 = (bf16[192,1024]{1,0:T(8,128)(2,1)}, bf16[192,1024]{1,0:T(8,128)(2,1)S(1)}, u32[]{:S(2)}) copy-start(bf16[192,1024]{1,0:T(8,128)(2,1)S(1)} %collective-permute-done.3.refs_3_) | copy-start | bytes 1179652
Sparse Core Ops, SparseCore 0:
  18.8 40.7 all-gather.2
where the time goes:
time: 106 us; the launch traced here: 105 us
  Pallas kernels  79 us (75%)
  between operations  14.2 us (13%)
  starting transfers between devices  5.28 us (5%)
  other arithmetic  4.68 us (4%)
  local copies, waits for them, and re-layouts  1.86 us (2%)
    pallas_call x5, Pallas kernels, prefill_part(): pl.pallas_call(functools.partial(prefill_kernel, tokens, first=first), gr...  68.2 us
    pallas_call x1, Pallas kernels, small_part(): pl.pallas_call(functools.partial(small_kernel, dec, over), grid_spec=pltp...  6.63 us
    ppermute x4, starting transfers between devices, per_device(): lax.ppermute(part, 'tensor', [(i, (i + shift) % ranks) for i in range(ran...  5.24 us
    pallas_call x1, Pallas kernels, finish_part(): pl.pallas_call(finish_kernel, grid_spec=pltpu.PrefetchScalarGridSpec(num_...  4.17 us
  transfers between devices with their start and end apart: 5, of which 0 were waited for; matrix products, arithmetic and copies ran while one was open for 1% of the time, Pallas kernels for 65%

commit v1 on v0

v1 whole, which is shorter than its diff:
```python
import functools
import math

import jax
import jax.numpy as jnp
from jax import lax
from jax.experimental import pallas as pl
from jax.experimental.pallas import tpu as pltpu
from jax.sharding import PartitionSpec as P

Q_HEADS = 64
KV_HEADS = 8
D_HEAD = 128
PAGE = 128
GROUP = Q_HEADS // KV_HEADS
SCALE = math.log2(math.e) / math.sqrt(D_HEAD)
LOW = -1e30
CHUNK = 512
VMEM_LIMIT = 60 * 2**20

NT = (((1,), (1,)), ((), ()))


def chunks_of(earlier, tail):
    starts = list(range(0, earlier, CHUNK)) + [earlier]
    return [(a, b - a) for a, b in zip(starts, starts[1:] + [earlier + tail])]


def prefill_kernel(
    tail, blk_ref, pages_ref, q_ref, k_hbm, v_hbm, o_ref,
    kbuf, vbuf, turned, score_a, score_b, top_a, top_b, sem, *, first, pack, turn
):
    heads = kbuf.shape[0]
    count = pages_ref.shape[0]
    span = count * PAGE
    rows = q_ref.shape[0]
    units = GROUP // pack
    pieces = chunks_of(span - tail, tail)

    def fetch(head):
        cols = pl.ds(pl.multiple_of((first + head) * D_HEAD, D_HEAD), D_HEAD)

        def one(j, _):
            src = pl.ds(pl.multiple_of(pages_ref[j] * PAGE, PAGE), PAGE)
            dst = pl.ds(pl.multiple_of(j * PAGE, PAGE), PAGE)
            pltpu.make_async_copy(k_hbm.at[src, cols], kbuf.at[head, dst], sem.at[head, 0]).start()
            pltpu.make_async_copy(v_hbm.at[src, cols], vbuf.at[head, dst], sem.at[head, 1]).start()
            return 0

        lax.fori_loop(0, count, one, 0)

    def keys_ready(head):
        pltpu.make_async_copy(kbuf.at[head], kbuf.at[head], sem.at[head, 0]).wait()
        if turn:

            def one(j, _):
                at = pl.ds(pl.multiple_of(j * PAGE, PAGE), PAGE)
                turned[:, at] = kbuf[head, at, :].T
                return 0

            lax.fori_loop(0, count, one, 0)

    def values_ready(head):
        pltpu.make_async_copy(vbuf.at[head], vbuf.at[head], sem.at[head, 1]).wait()

    def columns(unit, h):
        return pl.ds(pl.multiple_of((unit * pack + h) * D_HEAD, D_HEAD), D_HEAD)

    def across(x, size):
        return jnp.concatenate([x] * (size // D_HEAD), axis=1)

    def run(now, later):
        if later is not None:
            unit, score, top = later
            head = unit // units
            q = jnp.concatenate([q_ref[:, columns(unit, h)] for h in range(pack)], axis=0)
            best = None
        if now is not None:
            unit_now, score_now, top_now = now
            head_now = unit_now // units
            shift = top_now[...]
            acc = None
        for start, size in pieces:
            if later is not None:
                if turn:
                    s = jnp.dot(
                        q, turned[:, start:start + size], preferred_element_type=jnp.float32
                    )
                else:
                    keys = kbuf[head, start:start + size, :]
                    s = lax.dot_general(q, keys, NT, preferred_element_type=jnp.float32)
                if start >= span - tail:
                    usable = lax.broadcasted_iota(jnp.int32, (rows, size), 1) <= (
                        lax.broadcasted_iota(jnp.int32, (rows, size), 0) + blk_ref[0] * rows
                    )
                    s = jnp.where(usable[None], s.reshape(pack, rows, size), LOW).reshape(s.shape)
                score[:, start:start + size] = s
                for at in range(0, size, D_HEAD):
                    piece = s[:, at:at + D_HEAD]
                    best = piece if best is None else jnp.maximum(best, piece)
            if now is not None:
                p = jnp.exp2(score_now[:, start:start + size] * SCALE - across(shift, size))
                values = vbuf[head_now, start:start + size, :]
                wide = jnp.concatenate([values, jnp.ones_like(values)], axis=1)
                o = jnp.dot(p.astype(jnp.bfloat16), wide, preferred_element_type=jnp.float32)
                acc = o if acc is None else acc + o
        if later is not None:
            top[...] = jnp.broadcast_to(jnp.max(best, axis=1, keepdims=True) * SCALE, top.shape)
        if now is not None:
            o = (acc[:, :D_HEAD] / acc[:, D_HEAD:]).astype(o_ref.dtype)
            for h in range(pack):
                o_ref[:, columns(unit_now, h)] = o[h * rows:(h + 1) * rows]

    fetch(0)
    if heads > 1:
        fetch(1)
    keys_ready(0)
    a, b = (score_a, top_a), (score_b, top_b)
    run(None, (0, *a))
    values_ready(0)

    def body(i, _):
        u = 2 * i
        run((u, *a), (u + 1, *b))
        if heads > 1:
            head = (u + 2) // units

            @pl.when((u + 2) % units == 0)
            def _():
                @pl.when(head + 1 < heads)
                def _():
                    fetch(head + 1)

                keys_ready(head)
                values_ready(head)

        run((u + 1, *b), (u + 2, *a))
        return 0

    last = heads * units
    lax.fori_loop(0, last // 2 - 1, body, 0)
    run((last - 2, *a), (last - 1, *b))
    run((last - 1, *b), None)


def prefill_part(q, keys, values, pages, blk, ranks, first, heads, pack, turn, wide=False):
    tokens = q.shape[0]
    rows = tokens // ranks
    span = pages.shape[0] * PAGE
    width = heads * GROUP * D_HEAD
    total = ranks * keys.shape[1] // D_HEAD // heads if wide else 1
    work = heads * GROUP * rows * span

    return pl.pallas_call(
        functools.partial(prefill_kernel, tokens, first=first, pack=pack, turn=turn),
        grid_spec=pltpu.PrefetchScalarGridSpec(
            num_scalar_prefetch=2,
            grid=(1,),
            in_specs=[
                pl.BlockSpec((rows, width), lambda i, blk, pages: (blk[0], first // heads)),
                pl.BlockSpec(memory_space=pl.ANY),
                pl.BlockSpec(memory_space=pl.ANY),
            ],
            out_specs=pl.BlockSpec((rows, width), lambda i, blk, pages: (0, blk[0] if wide else 0)),
            scratch_shapes=[
                pltpu.VMEM((heads, span, D_HEAD), jnp.bfloat16),
                pltpu.VMEM((heads, span, D_HEAD), jnp.bfloat16),
                pltpu.VMEM((D_HEAD, span), jnp.bfloat16),
                pltpu.VMEM((pack * rows, span), jnp.float32),
                pltpu.VMEM((pack * rows, span), jnp.float32),
                pltpu.VMEM((pack * rows, D_HEAD), jnp.float32),
                pltpu.VMEM((pack * rows, D_HEAD), jnp.float32),
                pltpu.SemaphoreType.DMA((heads, 2)),
            ],
        ),
        out_shape=jax.ShapeDtypeStruct((rows, total * width), q.dtype),
        compiler_params=pltpu.CompilerParams(vmem_limit_bytes=VMEM_LIMIT),
        cost_estimate=pl.CostEstimate(
            flops=4 * work * D_HEAD,
            bytes_accessed=4 * (heads * span * D_HEAD + rows * width),
            transcendentals=work,
        ),
        name="prefill",
    )(blk, pages, q, keys, values)


def small_kernel(
    over_pages, dec_pages, over_len, dec_len, dest_ref, over_ref, decq_ref, k_hbm, v_hbm,
    dec_ref, out_ref, kbuf, vbuf, q_all, res, flat, sem
):
    over, (dec, per) = over_pages.shape[0], dec_pages.shape
    count = over + dec * per
    batch = q_all.shape[0]
    keys = count * PAGE
    heads = q_all.shape[1] // D_HEAD

    for j in range(count):
        page = over_pages[j] if j < over else dec_pages[(j - over) // per, (j - over) % per]
        src = pl.ds(pl.multiple_of(page * PAGE, PAGE), PAGE)
        dst = pl.ds(j * PAGE, PAGE)
        pltpu.make_async_copy(k_hbm.at[src], kbuf.at[dst], sem.at[0]).start()
        pltpu.make_async_copy(v_hbm.at[src], vbuf.at[dst], sem.at[1]).start()

    if batch > over + dec:
        q_all[...] = jnp.zeros_like(q_all)
    q_all[0:over, :] = over_ref[...].astype(jnp.float32)
    q_all[over:over + dec, :] = decq_ref[...].astype(jnp.float32)
    out_ref[...] = jnp.zeros_like(out_ref)
    row = lax.broadcasted_iota(jnp.int32, (batch, PAGE), 0)
    lane = lax.broadcasted_iota(jnp.int32, (batch, PAGE), 1)
    masks = []
    for j in range(count):
        owner, base = (j, 0) if j < over else (over + (j - over) // per, (j - over) % per * PAGE)
        most = over_len[j] if j < over else dec_len[owner - over]
        masks.append((row == owner) & (lane + base < most))
    pltpu.make_async_copy(kbuf, kbuf, sem.at[0]).wait()
    for g in range(k_hbm.shape[1] // D_HEAD):
        cols = slice(g * D_HEAD, (g + 1) * D_HEAD)
        q = jnp.concatenate(
            [q_all[:, (g * GROUP + h) * D_HEAD:(g * GROUP + h + 1) * D_HEAD] for h in range(GROUP)],
            axis=0,
        ).astype(jnp.bfloat16)
        s = lax.dot_general(q, kbuf[:, cols], NT, preferred_element_type=jnp.float32)
        s = s.reshape(GROUP, batch, keys)
        s = jnp.concatenate(
            [
                jnp.where(masks[j][None], s[:, :, j * PAGE:(j + 1) * PAGE], LOW)
                for j in range(count)
            ],
            axis=2,
        ).reshape(GROUP * batch, keys)
        p = jnp.exp2((s - jnp.max(s, axis=1, keepdims=True)) * SCALE)
        total = jnp.sum(p, axis=1, keepdims=True)
        w = (p / total).astype(jnp.bfloat16)
        if g == 0:
            pltpu.make_async_copy(vbuf, vbuf, sem.at[1]).wait()
        o = jnp.dot(w, vbuf[:, cols], preferred_element_type=jnp.float32)
        for h in range(GROUP):
            at = g * GROUP + h
            res[:, at * D_HEAD:(at + 1) * D_HEAD] = o[h * batch:(h + 1) * batch]
            flat[pl.ds(at, batch, stride=heads), :] = o[h * batch:(h + 1) * batch]
    dec_ref[...] = res[over:over + dec, :].astype(dec_ref.dtype)
    for m in range(over):
        out_ref[dest_ref[m]] = flat[m * heads:(m + 1) * heads, :].astype(out_ref.dtype)


def small_part(decode_q, overflow_q, keys, values, dec_pages, over_pages, dec_len, over_len, dest, replicas):
    dec, over = decode_q.shape[0], overflow_q.shape[0]
    batch = -(-(dec + over) // 8) * 8
    width = decode_q.shape[1]
    span = (over + dec_pages.size) * PAGE
    work = batch * width * span
    moved = (replicas, width // D_HEAD, D_HEAD)
    return pl.pallas_call(
        small_kernel,
        grid_spec=pltpu.PrefetchScalarGridSpec(
            num_scalar_prefetch=5,
            grid=(1,),
            in_specs=[
                pl.BlockSpec((over, width), lambda i, *_: (0, 0)),
                pl.BlockSpec((dec, width), lambda i, *_: (0, 0)),
                pl.BlockSpec(memory_space=pl.ANY),
                pl.BlockSpec(memory_space=pl.ANY),
            ],
            out_specs=[
                pl.BlockSpec((dec, width), lambda i, *_: (0, 0)),
                pl.BlockSpec(moved, lambda i, *_: (0, 0, 0)),
            ],
            scratch_shapes=[
                pltpu.VMEM((span, keys.shape[1]), jnp.bfloat16),
                pltpu.VMEM((span, keys.shape[1]), jnp.bfloat16),
                pltpu.VMEM((batch, width), jnp.float32),
                pltpu.VMEM((batch, width), jnp.float32),
                pltpu.VMEM((batch * width // D_HEAD, D_HEAD), jnp.float32),
                pltpu.SemaphoreType.DMA((2,)),
            ],
        ),
        out_shape=[
            jax.ShapeDtypeStruct((dec, width), decode_q.dtype),
            jax.ShapeDtypeStruct(moved, decode_q.dtype),
        ],
        compiler_params=pltpu.CompilerParams(vmem_limit_bytes=VMEM_LIMIT),
        cost_estimate=pl.CostEstimate(
            flops=4 * work, bytes_accessed=4 * span * keys.shape[1], transcendentals=work // D_HEAD
        ),
        name="small",
    )(over_pages, dec_pages, over_len, dec_len, dest, overflow_q, decode_q, keys, values)


def finish_kernel(ranks, rank_ref, rows_ref, big_ref, *refs):
    got, (out_ref, mov_ref, flat, sem) = refs[:-4], refs[-4:]
    del big_ref
    cols = GROUP * D_HEAD
    heads = len(got) // (ranks - 1)
    copies = []
    for i, part in enumerate(got):
        source = lax.rem(rank_ref[0] + ranks - (i // heads + 1), ranks)
        to = pl.ds(pl.multiple_of((source * heads + i % heads) * cols, cols), cols)
        copies.append(pltpu.make_async_copy(part, out_ref.at[:, to], sem.at[i]))
        copies[-1].start()
    replicas, count, _ = rows_ref.shape
    flat[...] = rows_ref[...].astype(jnp.float32).reshape(flat.shape)
    for h in range(count):
        line = flat[pl.ds(h, replicas, stride=count), :]
        mov_ref[:, h * D_HEAD:(h + 1) * D_HEAD] = line.astype(mov_ref.dtype)
    for copy in copies:
        copy.wait()


def finish_part(rank, ranks, rows, big, got):
    replicas, count, _ = rows.shape
    anywhere = pl.BlockSpec(memory_space=pl.ANY)
    return pl.pallas_call(
        functools.partial(finish_kernel, ranks),
        grid_spec=pltpu.PrefetchScalarGridSpec(
            num_scalar_prefetch=1,
            grid=(1,),
            in_specs=[pl.BlockSpec(rows.shape, lambda i, *_: (0, 0, 0)), anywhere]
            + [pl.BlockSpec(memory_space=pltpu.VMEM)] * len(got),
            out_specs=[anywhere, pl.BlockSpec((replicas, count * D_HEAD), lambda i, *_: (0, 0))],
            scratch_shapes=[
                pltpu.VMEM((replicas * count, D_HEAD), jnp.float32),
                pltpu.SemaphoreType.DMA((len(got),)),
            ],
        ),
        out_shape=[
            jax.ShapeDtypeStruct(big.shape, big.dtype),
            jax.ShapeDtypeStruct((replicas, count * D_HEAD), big.dtype),
        ],
        input_output_aliases={2: 0},
        compiler_params=pltpu.CompilerParams(vmem_limit_bytes=VMEM_LIMIT),
        cost_estimate=pl.CostEstimate(
            flops=0, bytes_accessed=2 * big.size + 4 * rows.size, transcendentals=0
        ),
        name="finish",
    )(rank, rows, big, *got)


def per_device(
    prefill_q,
    decode_q,
    overflow_q,
    key_pool,
    value_pool,
    prefill_pages,
    decode_pages,
    decode_len,
    overflow_pages,
    overflow_len,
    overflow_dest,
):
    ranks, replicas = lax.axis_size("tensor"), lax.axis_size("replica")
    rank = lax.axis_index("tensor")
    heads = key_pool.shape[1] // D_HEAD
    pages = prefill_pages[0]

    decode_out, sent = small_part(
        decode_q,
        overflow_q,
        key_pool,
        value_pool,
        decode_pages,
        overflow_pages,
        decode_len,
        overflow_len,
        overflow_dest,
        replicas,
    )
    rows = lax.all_to_all(sent, "replica", split_axis=0, concat_axis=0, tiled=True)

    got = []
    for shift in range(1, ranks):
        blk = lax.rem(rank + shift, ranks)[None].astype(jnp.int32)
        for g in range(heads):
            part = prefill_part(
                prefill_q, key_pool, value_pool, pages, blk, ranks, g, 1, pack=2, turn=True
            )
            got.append(lax.ppermute(part, "tensor", [(i, (i + shift) % ranks) for i in range(ranks)]))
    own = rank[None].astype(jnp.int32)
    prefill_out = prefill_part(
        prefill_q, key_pool, value_pool, pages, own, ranks, 0, heads, pack=4, turn=False, wide=True
    )
    prefill_out, moved_out = finish_part(own, ranks, rows, prefill_out, got)
    return (prefill_out, decode_out, moved_out)


def solution(mesh):
    in_specs = (
        P("replica", "tensor"),
        P("replica", "tensor"),
        P("replica", "tensor"),
        P("replica", "tensor"),
        P("replica", "tensor"),
        P("replica", None),
        P("replica", None),
        P("replica"),
        P("replica"),
        P("replica"),
        P("replica"),
    )
    out_specs = (P(("replica", "tensor"), None), P("replica", "tensor"), P("replica", "tensor"))
    return jax.shard_map(
        per_device, mesh=mesh, in_specs=in_specs, out_specs=out_specs, check_vma=False
    )
```

time: 106 us -> 96.1 us (0.907)
  between operations: 14.2 us -> 0.95 us
  starting transfers between devices: 5.28 us -> 11.7 us
  other arithmetic: 4.68 us -> 0 us
  Pallas kernels: 79 us -> 80.7 us
    all_to_all x0 -> x1, starting transfers between devices: none -> 7.39 us  [per_device(): lax.all_to_all(sent, 'replica', split_axis=0, concat_axis=0, tiled=True)]
    concatenate x2 -> x0, other arithmetic: 2.52 us -> none  [the longest x1 1.28 us: per_device(): jnp.concatenate([overflow_len, decode_len])]
    pallas_call x7, Pallas kernels: 79 us -> 80.7 us  [the longest x5 70.8 us: prefill_part(): pl.pallas_call(functools.partial(prefill_kernel, tokens, first=first, pac...]
    convert_element_type x1 -> x0, other arithmetic: 1.54 us -> none  [small_part(): q = jnp.concatenate([overflow_q, decode_q], axis=0).astype(jnp.float32)]
  transfers between devices with their start and end apart: 5 -> 5, of which waited for: 0 -> 0; matrix products, arithmetic and copies ran while one was open for 1% -> 0% of each run, Pallas kernels for 65% -> 74%
where the time goes in v1:
time: 96.1 us; the launch traced here: 95.1 us
  Pallas kernels  80.7 us (84%)
  starting transfers between devices  11.7 us (12%)
  local copies, waits for them, and re-layouts  1.75 us (2%)
    pallas_call x5, Pallas kernels, prefill_part(): pl.pallas_call(functools.partial(prefill_kernel, tokens, first=first, pac...  70.8 us
    all_to_all x1, starting transfers between devices, per_device(): lax.all_to_all(sent, 'replica', split_axis=0, concat_axis=0, tiled=True)  7.39 us
    pallas_call x1, Pallas kernels, small_part(): pl.pallas_call(small_kernel, grid_spec=pltpu.PrefetchScalarGridSpec(num_s...  6.63 us
    ppermute x4, starting transfers between devices, per_device(): lax.ppermute(part, 'tensor', [(i, (i + shift) % ranks) for i in range(ran...  4.31 us
    pallas_call x1, Pallas kernels, finish_part(): pl.pallas_call(functools.partial(finish_kernel, ranks), grid_spec=pltpu.P...  3.22 us
  transfers between devices with their start and end apart: 5, of which 0 were waited for; matrix products, arithmetic and copies ran while one was open for 0% of the time, Pallas kernels for 74%

profile of v1, /device:TPU:0, one launch (start us, length us, event | category | flops | bytes accessed | tf_op | source)
XLA Modules:
  0.0 95.1 jit_solution(7368990918958572689)
XLA Ops:
  0.6 6.6 %small.1 = (bf16[2,4096]{1,0:T(2,128)(2,1)}, bf16[16,32,128]{2,1,0:T(8,128)(2,1)}) custom-call(s32[6]{0:T(128)} %over_pages.1, s32[2,4]{1,0:T(2,128)} %dec_pages.1, s32[6]{0:T(128)} %over_len.1, s32[2]{0:T(128)} %dec_len.1, s32[6]{0:T(128)} %dest_ref.1, bf16[6,4096]{1,0:T(8,128)(2,1)} %over_ref.1, bf16[2,4096]{1,0:T(2,128)(2,1)} %decq_ref.1, ...), custom_call_target="tpu_custom_call" | custom-call | flops 234881024 | bytes 3670016 | tf_op jit(solution)/shard_map/small/pallas_call | solution.py:254
  7.3 7.4 %all-to-all-start = ((bf16[16,32,128]{2,1,0:T(8,128)(2,1)}), bf16[16,32,128]{2,1,0:T(8,128)(2,1)S(1)}, u32[]{:S(2)}, u32[]{:S(2)}) async-start(bf16[16,32,128]{2,1,0:T(8,128)(2,1)} %get-tuple-element.7), calls=%async_computation | async-start | bytes 262144 | tf_op jit(solution)/shard_map/all_to_all | solution.py:369
  14.7 10.5 %prefill.6 = bf16[192,1024]{1,0:T(8,128)(2,1)} custom-call(s32[1]{0:T(128)} %bitcast.2.blk_ref, s32[19]{0:T(128)} %bitcast.3, bf16[384,4096]{1,0:T(8,128)(2,1)} %q_ref.9, bf16[4224,512]{1,0:T(8,128)(2,1)} %k_hbm.11, bf16[4224,512]{1,0:T(8,128)(2,1)} %v_hbm.11), custom_call_target="tpu_custom_call" | custom-call | flops 1912602624 | bytes 2031616 | tf_op jit(solution)/shard_map/prefill/pallas_call | solution.py:154
  25.2 1.6 %collective-permute-start = (bf16[192,1024]{1,0:T(8,128)(2,1)}, bf16[192,1024]{1,0:T(8,128)(2,1)S(1)}, u32[]{:S(2)}, u32[]{:S(2)}) collective-permute-start(bf16[192,1024]{1,0:T(8,128)(2,1)} %prefill.6), channel_id=1, source_target_pairs={{0,1},{1,0},{2,3},{3,2},{4,5},{5,4},{6,7},{7,6},{8,9},{9,8},{10,11... | collective-permute-start | bytes 1179656 | tf_op jit(solution)/shard_map/ppermute | solution.py:378
  26.8 10.5 %prefill.7 = bf16[192,1024]{1,0:T(8,128)(2,1)} custom-call(s32[1]{0:T(128)} %bitcast.2.blk_ref, s32[19]{0:T(128)} %bitcast.4, bf16[384,4096]{1,0:T(8,128)(2,1)} %q_ref.9, bf16[4224,512]{1,0:T(8,128)(2,1)} %k_hbm.11, bf16[4224,512]{1,0:T(8,128)(2,1)} %v_hbm.11), custom_call_target="tpu_custom_call" | custom-call | flops 1912602624 | bytes 2031616 | tf_op jit(solution)/shard_map/prefill/pallas_call | solution.py:154
  37.3 0.6 collective-permute-start.1
  37.9 10.7 %prefill.8 = bf16[192,1024]{1,0:T(8,128)(2,1)} custom-call(s32[1]{0:T(128)} %bitcast.2.blk_ref, s32[19]{0:T(128)} %bitcast.5, bf16[384,4096]{1,0:T(8,128)(2,1)} %q_ref.9, bf16[4224,512]{1,0:T(8,128)(2,1)} %k_hbm.11, bf16[4224,512]{1,0:T(8,128)(2,1)} %v_hbm.11), custom_call_target="tpu_custom_call" | custom-call | flops 1912602624 | bytes 2031616 | tf_op jit(solution)/shard_map/prefill/pallas_call | solution.py:154
  48.6 1.6 %collective-permute-start.2 = (bf16[192,1024]{1,0:T(8,128)(2,1)}, bf16[192,1024]{1,0:T(8,128)(2,1)S(1)}, u32[]{:S(2)}, u32[]{:S(2)}) collective-permute-start(bf16[192,1024]{1,0:T(8,128)(2,1)} %prefill.8), channel_id=1, source_target_pairs={{0,1},{1,0},{2,3},{3,2},{4,5},{5,4},{6,7},{7,6},{8,9},{9,8},{10,11... | collective-permute-start | bytes 1179656 | tf_op jit(solution)/shard_map/ppermute | solution.py:378
  50.2 10.5 %prefill.9 = bf16[192,1024]{1,0:T(8,128)(2,1)} custom-call(s32[1]{0:T(128)} %bitcast.2.blk_ref, s32[19]{0:T(128)} %bitcast.6, bf16[384,4096]{1,0:T(8,128)(2,1)} %q_ref.9, bf16[4224,512]{1,0:T(8,128)(2,1)} %k_hbm.11, bf16[4224,512]{1,0:T(8,128)(2,1)} %v_hbm.11), custom_call_target="tpu_custom_call" | custom-call | flops 1912602624 | bytes 2031616 | tf_op jit(solution)/shard_map/prefill/pallas_call | solution.py:154
  60.7 0.6 collective-permute-start.3
  61.3 28.5 %prefill.5.big_ref = bf16[192,8192]{1,0:T(8,128)(2,1)} custom-call(s32[1]{0:T(128)} %bitcast.blk_ref.rank_ref, s32[19]{0:T(128)} %bitcast.7, bf16[384,4096]{1,0:T(8,128)(2,1)} %q_ref.9, bf16[4224,512]{1,0:T(8,128)(2,1)} %k_hbm.11, bf16[4224,512]{1,0:T(8,128)(2,1)} %v_hbm.11), custom_call_target="tpu_custom_call" | custom-call | flops 7650410496 | bytes 8126464 | tf_op jit(solution)/shard_map/prefill/pallas_call | solution.py:154
  89.8 0.0 all-to-all-done.rows_ref
  89.9 0.0 copy-start
  89.9 0.0 collective-permute-done.refs_0_
  89.9 0.0 copy-start.1
  89.9 0.0 collective-permute-done.1.refs_1_
  89.9 0.0 copy-start.2
  89.9 0.0 collective-permute-done.2.refs_2_
  89.9 0.0 copy-start.3
  89.9 0.0 collective-permute-done.3.refs_3_
  89.9 0.6 copy-done
  90.5 0.1 copy-done.1
  90.6 0.1 copy-done.2
  90.8 0.1 copy-done.3
  90.9 0.0 copy-start.4
  90.9 0.7 copy-done.4
  91.7 3.2 %finish.1 = (bf16[192,8192]{1,0:T(8,128)(2,1)}, bf16[16,4096]{1,0:T(8,128)(2,1)}) custom-call(s32[1]{0:T(128)} %bitcast.blk_ref.rank_ref, bf16[16,32,128]{2,1,0:T(8,128)(2,1)} %copy-done, bf16[192,8192]{1,0:T(8,128)(2,1)} %prefill.5.big_ref, bf16[192,1024]{1,0:T(8,128)(2,1)} %copy-done.1, ...), custom_call_target="tpu_custom_call", output_to_operand_aliasing={{0}: (2, {})} | custom-call | bytes 3407872 | tf_op jit(solution)/shard_map/finish/pallas_call | solution.py:313
Async XLA Ops:
  7.3 82.6 %all-to-all-start = ((bf16[16,32,128]{2,1,0:T(8,128)(2,1)}), bf16[16,32,128]{2,1,0:T(8,128)(2,1)S(1)}, u32[]{:S(2)}, u32[]{:S(2)}) async-start(bf16[16,32,128]{2,1,0:T(8,128)(2,1)} %get-tuple-element.7), calls=%async_computation | async-start | bytes 262144 | tf_op jit(solution)/shard_map/all_to_all | solution.py:369
  25.2 64.7 %collective-permute-start = (bf16[192,1024]{1,0:T(8,128)(2,1)}, bf16[192,1024]{1,0:T(8,128)(2,1)S(1)}, u32[]{:S(2)}, u32[]{:S(2)}) collective-permute-start(bf16[192,1024]{1,0:T(8,128)(2,1)} %prefill.6), channel_id=1, source_target_pairs={{0,1},{1,0},{2,3},{3,2},{4,5},{5,4},{6,7},{7,6},{8,9},{9,8},{10,11... | collective-permute-start | bytes 1179656 | tf_op jit(solution)/shard_map/ppermute | solution.py:378
  37.3 52.6 %collective-permute-start.1 = (bf16[192,1024]{1,0:T(8,128)(2,1)}, bf16[192,1024]{1,0:T(8,128)(2,1)S(1)}, u32[]{:S(2)}, u32[]{:S(2)}) collective-permute-start(bf16[192,1024]{1,0:T(8,128)(2,1)} %prefill.7), channel_id=1, source_target_pairs={{0,1},{1,0},{2,3},{3,2},{4,5},{5,4},{6,7},{7,6},{8,9},{9,8},{10,11... | collective-permute-start | bytes 1179656 | tf_op jit(solution)/shard_map/ppermute | solution.py:378
  48.6 41.3 %collective-permute-start.2 = (bf16[192,1024]{1,0:T(8,128)(2,1)}, bf16[192,1024]{1,0:T(8,128)(2,1)S(1)}, u32[]{:S(2)}, u32[]{:S(2)}) collective-permute-start(bf16[192,1024]{1,0:T(8,128)(2,1)} %prefill.8), channel_id=1, source_target_pairs={{0,1},{1,0},{2,3},{3,2},{4,5},{5,4},{6,7},{7,6},{8,9},{9,8},{10,11... | collective-permute-start | bytes 1179656 | tf_op jit(solution)/shard_map/ppermute | solution.py:378
  60.7 29.2 %collective-permute-start.3 = (bf16[192,1024]{1,0:T(8,128)(2,1)}, bf16[192,1024]{1,0:T(8,128)(2,1)S(1)}, u32[]{:S(2)}, u32[]{:S(2)}) collective-permute-start(bf16[192,1024]{1,0:T(8,128)(2,1)} %prefill.9), channel_id=1, source_target_pairs={{0,1},{1,0},{2,3},{3,2},{4,5},{5,4},{6,7},{7,6},{8,9},{9,8},{10,11... | collective-permute-start | bytes 1179656 | tf_op jit(solution)/shard_map/ppermute | solution.py:378
  89.9 0.6 copy-start
  89.9 0.8 copy-start.1
  89.9 0.9 copy-start.2
  89.9 1.0 %copy-start.3 = (bf16[192,1024]{1,0:T(8,128)(2,1)}, bf16[192,1024]{1,0:T(8,128)(2,1)S(1)}, u32[]{:S(2)}) copy-start(bf16[192,1024]{1,0:T(8,128)(2,1)S(1)} %collective-permute-done.2.refs_2_) | copy-start | bytes 1179652
  90.9 0.7 copy-start.4
